TPU v7x, 32 devices: a whole 2x2x4 slice. The times are simulated.
32 devices in a mesh: row: 4 (over z), col: 8 (over y, x, core).
Axes of the slice: x: 2, y: 2, z: 4, core: 2. Of those that a mesh axis runs over, the one named last changes fastest.
Arguments:
- panel: bfloat16 [16, 1024, 256], P('row', 'col'), may hold values from -6 to 6
- inverse_factor: bfloat16 [1024, 1024], P('row', 'col'), as said below
- ranks: int32 [16], replicated, may hold values from 32 to 256
Outputs:
- solved: bfloat16 [16, 1024, 256], P('row', 'col')
- core_blocks: bfloat16 [16, 16, 256, 256], P('row', 'col')
Inputs may be any that keep to these rules, and one draw needn't show every extreme that they name: inverse_factor is lower triangular with a diagonal between 0.5 and 3.
All inputs are finite; a program needn't handle non-finite values.
Results may differ from a plain program's by a relative error of at most 0.017.
Values may be sent and summed in bfloat16 or wider, within the bound.
A program may use at most 64 MiB of HBM per device.

v0:
```python
import functools

import jax
import jax.numpy as jnp
from jax import lax
from jax.experimental import pallas as pl
from jax.experimental.pallas import tpu as pltpu
from jax.sharding import PartitionSpec as P

MESH = pl.DeviceIdType.MESH
FLIPS = (1, 2, 4)


def spread(value, axis, source):
    kept = jnp.where(lax.axis_index(axis) == source, value, 0).astype(value.dtype)
    return lax.psum(kept, axis)


def per_device(panel, inverse_factor, ranks):
    tile_count = panel.shape[0]
    row_part = panel.shape[1]
    rank_width = panel.shape[2]
    row_index = lax.axis_index("row")
    col_index = lax.axis_index("col")
    col_count = lax.axis_size("col")
    row_count = lax.axis_size("row")
    factor_cols = lax.all_gather(inverse_factor, "row", axis=0, tiled=True)
    own_ranks = lax.dynamic_slice_in_dim(ranks, row_index * tile_count, tile_count, 0)
    column_ids = jnp.arange(rank_width, dtype=jnp.int32)
    keep_cols = (column_ids[None, :] < own_ranks[:, None]).astype(jnp.bfloat16)
    masked = panel * keep_cols[:, None, :]
    partial_value = jnp.einsum(
        "ab,tbr->tar", factor_cols, masked, preferred_element_type=jnp.float32
    )
    summed = lax.psum(partial_value.astype(jnp.bfloat16), "col")
    solved_own = lax.dynamic_slice_in_dim(summed, col_index * row_part, row_part, 1)
    tiles_per_col = tile_count * row_count // col_count
    first_tile = col_index * tiles_per_col
    source = first_tile // tile_count
    offset = first_tile % tile_count
    picked = lax.dynamic_slice_in_dim(summed, offset, tiles_per_col, 0)
    col_tiles = spread(picked, "row", source)
    core_blocks = jnp.einsum(
        "tar,uas->turs", summed, col_tiles, preferred_element_type=jnp.float32
    ).astype(jnp.bfloat16)
    return (solved_own, core_blocks)


def kernel(
    rows, cols, ranks_hbm, p_hbm, f_hbm, o_ref, core_ref,
    ranks_ref, p_ref, fb, pb, cb, pt, srt, wt, acc,
    recv, send, zf_send, zc_recv, zc_send, loc, fetch,
):
    z = lax.axis_index("row")
    c = lax.axis_index("col")
    tiles, pr, width = p_ref.shape
    fr, fc = f_hbm.shape
    per = tiles * rows // cols
    groups = tiles // per
    source = (c * per) // tiles
    group = ((c * per) % tiles) // per

    def at(m):
        out = c
        for bit in FLIPS:
            if (m // bit) % 2:
                out = out + bit * (1 - 2 * ((c // bit) % 2))
        return out

    up, down = z + 1 < rows, z >= 1

    fetches = (
        pltpu.make_async_copy(ranks_hbm, ranks_ref, fetch.at[0]),
        pltpu.make_async_copy(
            f_hbm,
            fb.at[c, pl.ds(pl.multiple_of(z * fr, fr), fr)],
            fetch.at[1],
        ),
        pltpu.make_async_copy(p_hbm, p_ref, fetch.at[2]),
    )
    for copy in fetches:
        copy.start()

    barrier = pltpu.get_barrier_semaphore()
    for bit in FLIPS:
        pl.semaphore_signal(barrier, inc=1, device_id=(z, at(bit)), device_id_type=MESH)

    @pl.when(up)
    def _():
        pl.semaphore_signal(barrier, inc=1, device_id=(z + 1, c), device_id_type=MESH)

    @pl.when(down)
    def _():
        pl.semaphore_signal(barrier, inc=1, device_id=(z - 1, c), device_id_type=MESH)

    def f_view(s, j):
        return fb.at[s, pl.ds(pl.multiple_of(j * fr, fr), fr)]

    def p_view(s, g):
        return pb.at[pl.ds(g * per, per), pl.ds(pl.multiple_of(s * pr, pr), pr), :]

    def p_tile(s, u):
        return pb.at[group * per + u, pl.ds(pl.multiple_of(s * pr, pr), pr), :]

    def c_tile(s, u):
        return cb.at[u, pl.ds(pl.multiple_of(s * pr, pr), pr), :]

    def exists(s, j):
        return (j + 1) * fr > s * fc

    def flip_copy(view, m, item, way):
        return pltpu.make_async_remote_copy(
            src_ref=view, dst_ref=view,
            send_sem=send.at[m // 2, item, way], recv_sem=recv.at[m ^ FLIPS[way], item],
            device_id=(z, at(FLIPS[way])), device_id_type=MESH,
        )

    def act(copy, start):
        if start:
            copy.start()
        else:
            copy.wait_send()

    def wait_recv(view, m, item):
        pltpu.make_async_remote_copy(
            src_ref=view, dst_ref=view,
            send_sem=send.at[0, item, 0], recv_sem=recv.at[m, item],
            device_id=(z, at(1)), device_id_type=MESH,
        ).wait_recv()

    def f_forward(m, j, start=True):
        view = f_view(at(m), j)
        if m == 0:
            act(flip_copy(view, m, j, 1), start)
            act(flip_copy(view, m, j, 2), start)
        elif m == 2:
            @pl.when(j % 2 == 0)
            def _():
                act(flip_copy(view, m, j, 2), start)
        elif m == 4:
            @pl.when(j % 2 == 1)
            def _():
                act(flip_copy(view, m, j, 1), start)
        act(flip_copy(view, m, j, 0), start)

    def p_forward(m, g, start=True):
        view = p_view(at(m), g)
        item = rows + g
        if m == 0:
            act(flip_copy(view, m, item, 1), start)
            act(flip_copy(view, m, item, 2), start)
        elif m == 2 and g % 2 == 0:
            act(flip_copy(view, m, item, 2), start)
        elif m == 4 and g % 2 == 1:
            act(flip_copy(view, m, item, 1), start)
        act(flip_copy(view, m, item, 0), start)

    def zf(j, start=True):
        view = f_view(c, j)
        for way, (go, to) in enumerate((((z >= j) & up, z + 1), ((z <= j) & down, z - 1))):
            @pl.when(go)
            def _():
                act(pltpu.make_async_remote_copy(
                    src_ref=view, dst_ref=view,
                    send_sem=zf_send.at[j, way], recv_sem=recv.at[0, j],
                    device_id=(to, c), device_id_type=MESH,
                ), start)

    def zc(m, u, view, start=True):
        for way, (go, to) in enumerate((((z >= source) & up, z + 1), ((z <= source) & down, z - 1))):
            @pl.when(go)
            def _():
                act(pltpu.make_async_remote_copy(
                    src_ref=view, dst_ref=c_tile(at(m), u),
                    send_sem=zc_send.at[m, u, way], recv_sem=zc_recv.at[m, u],
                    device_id=(to, c), device_id_type=MESH,
                ), start)

    def own_copy(m, u):
        return pltpu.make_async_copy(p_tile(at(m), u), c_tile(at(m), u), loc.at[m, u])

    def from_source(m):
        @pl.when(z == source)
        def _():
            for u in range(per):
                zc(m, u, p_tile(at(m), u))
            for u in range(per):
                own_copy(m, u).start()

    def relay(m):
        @pl.when(z != source)
        def _():
            for u in range(per):
                view = c_tile(at(m), u)
                pltpu.make_async_remote_copy(
                    src_ref=view, dst_ref=view,
                    send_sem=zc_send.at[m, u, 0], recv_sem=zc_recv.at[m, u],
                    device_id=(z, at(1)), device_id_type=MESH,
                ).wait_recv()
                zc(m, u, view)

    for copy in fetches:
        copy.wait()
    lanes = lax.broadcasted_iota(jnp.int32, (pr, width), 1)
    for t in range(tiles):
        keep = lanes < ranks_ref[z * tiles + t]
        pb[t, pl.ds(pl.multiple_of(c * pr, pr), pr), :] = jnp.where(
            keep, p_ref[t].astype(jnp.float32), 0.0
        ).astype(pb.dtype)

    pl.semaphore_wait(barrier, len(FLIPS) + jnp.where(up, 1, 0) + jnp.where(down, 1, 0))

    @pl.when(exists(c, z))
    def _():
        zf(z)
        f_forward(0, z)

    from_source(0)
    for g in range(groups):
        p_forward(0, g)

    def near_first(body):
        for d in range(1, rows):
            for j in (z + d, z - d):
                @pl.when((j >= 0) & (j < rows))
                def _():
                    @pl.when(exists(c, j))
                    def _():
                        body(j)

    def f_along(j):
        wait_recv(f_view(c, j), 0, j)
        zf(j)
        f_forward(0, j)

    near_first(f_along)

    def p_arrive(m):
        for g in range(groups):
            wait_recv(p_view(at(m), g), m, rows + g)
            if m % 2 == 0:
                p_forward(m, g)
        from_source(m)

    def f_arrive(m):
        def one(d, carry):
            j = (z + d) % rows

            @pl.when(exists(at(m), j))
            def _():
                wait_recv(f_view(at(m), j), m, j)
                if m % 2 == 0:
                    f_forward(m, j)

            return carry

        lax.fori_loop(0, rows, one, 0)

    def flip(m):
        s = at(m)
        for t in range(tiles):
            piece = pb[t, pl.ds(pl.multiple_of(s * pr, pr), pr), :]
            pt[t * width : (t + 1) * width, pl.ds(pl.multiple_of(s * pr, pr), pr)] = piece.T

    def solve_rows(i):
        high = (i + 1) * fr
        srt[:, i * fr : high] = lax.dot_general(
            pt[:, :high],
            jnp.concatenate([fb[k, i * fr : high] for k in range(high // fc)], axis=1),
            (((1,), (1,)), ((), ())),
            preferred_element_type=jnp.float32,
        ).astype(srt.dtype)

    def weigh(i):
        wt[i] = jnp.dot(
            srt[:, i * fr :],
            jnp.concatenate(
                [fb[k, i * fr :] for k in range(i * fr // fc, (i + 1) * fr // fc)], axis=1
            ),
            preferred_element_type=jnp.float32,
        ).astype(wt.dtype)

    pieces = fr // pr
    last = cols - pieces

    def add_cores(m):
        q = at(m) // pieces

        @pl.when(z == source)
        def _():
            for k in range(pieces):
                for u in range(per):
                    own_copy(m + k, u).wait()

        for u in range(per):
            part = jnp.dot(
                wt[q], cb[u, pl.ds(pl.multiple_of(q * fr, fr), fr), :],
                preferred_element_type=jnp.float32,
            )
            if m == 0:
                acc[u] = part
            elif m < last:
                acc[u] += part
            else:
                total = (acc[u] + part).astype(core_ref.dtype)
                for t in range(tiles):
                    core_ref[t, u] = total[t * width : (t + 1) * width]

    flip(0)
    p_arrive(1)
    relay(0)
    flip(1)
    p_arrive(2)
    p_arrive(4)
    relay(1)
    p_arrive(3)
    f_arrive(2)
    f_arrive(4)
    relay(2)
    for m in (2, 3, 4):
        flip(m)
    p_arrive(5)
    p_arrive(6)
    f_arrive(6)
    relay(4)
    flip(5)
    flip(6)
    p_arrive(7)
    flip(7)
    for m in (1, 3, 5, 7):
        f_arrive(m)
    relay(3)
    for i in range(rows):
        solve_rows(i)
        if i == rows // 2 - 1:
            relay(5)
    for t in range(tiles):
        o_ref[t] = srt[t * width : (t + 1) * width, pl.ds(pl.multiple_of(c * pr, pr), pr)].T
    relay(6)
    for i in range(rows):
        weigh(i)
    passes = ((z > source) & up) | ((z < source) & down)

    def add_early():
        for m in range(0, last, pieces):
            add_cores(m)

    pl.when(jnp.logical_not(passes))(add_early)
    relay(7)
    pl.when(passes)(add_early)
    add_cores(last)

    @pl.when(exists(c, z))
    def _():
        zf(z, start=False)
        f_forward(0, z, start=False)

    def f_along_left(j):
        zf(j, start=False)
        f_forward(0, j, start=False)

    near_first(f_along_left)
    for m in range(0, cols, 2):
        for g in range(groups):
            p_forward(m, g, start=False)
        if m:
            def one(j, carry, m=m):
                @pl.when(exists(at(m), j))
                def _():
                    f_forward(m, j, start=False)

                return carry

            lax.fori_loop(0, rows, one, 0)
    for m in range(cols):
        for u in range(per):
            @pl.when(z == source)
            def _():
                zc(m, u, p_tile(at(m), u), start=False)

            @pl.when(z != source)
            def _():
                zc(m, u, c_tile(at(m), u), start=False)


def fits(rows, cols, panel, factor):
    tiles, pr, width = panel.shape
    fr, fc = factor.shape
    per = tiles * rows // cols
    return (
        cols == 2 ** len(FLIPS)
        and rows > 1
        and per > 0
        and tiles == 2 * per
        and pr == fc
        and pr % 16 == 0
        and fr == 2 * fc
        and fc % 128 == 0
        and width % 128 == 0
        and rows * fr == cols * fc
    )


def on_device(rows, cols, panel, factor, ranks):
    if not fits(rows, cols, panel, factor):
        return per_device(panel, factor, ranks)
    tiles, pr, width = panel.shape
    fr, fc = factor.shape
    order = rows * fr
    per = tiles * rows // cols
    items = rows + tiles // per
    vmem = pl.BlockSpec(memory_space=pltpu.VMEM)
    dma = pltpu.SemaphoreType.DMA
    kept = panel.dtype
    return tuple(pl.pallas_call(
        functools.partial(kernel, rows, cols),
        out_shape=(
            jax.ShapeDtypeStruct(panel.shape, kept),
            jax.ShapeDtypeStruct((tiles, per, width, width), kept),
        ),
        in_specs=[pl.BlockSpec(memory_space=pltpu.HBM)] * 3,
        out_specs=(vmem, vmem),
        scratch_shapes=[
            pltpu.SMEM(ranks.shape, ranks.dtype),
            pltpu.VMEM(panel.shape, kept),
            pltpu.VMEM((cols, order, fc), kept),
            pltpu.VMEM((tiles, order, width), kept),
            pltpu.VMEM((per, order, width), kept),
            pltpu.VMEM((tiles * width, order), kept),
            pltpu.VMEM((tiles * width, order), kept),
            pltpu.VMEM((rows, tiles * width, fr), kept),
            pltpu.VMEM((per, tiles * width, width), jnp.float32),
            dma((cols, items)),
            dma((cols // 2, items, len(FLIPS))),
            dma((rows, 2)),
            dma((cols, per)),
            dma((cols, per, 2)),
            dma((cols, per)),
            dma((3,)),
        ],
        compiler_params=pltpu.CompilerParams(
            collective_id=0, has_side_effects=True, vmem_limit_bytes=40 * 2**20
        ),
    )(ranks, panel, factor))


def solution(mesh):
    return jax.shard_map(
        functools.partial(on_device, mesh.shape["row"], mesh.shape["col"]),
        mesh=mesh,
        in_specs=(P("row", "col", None), P("row", "col"), P()),
        out_specs=(P("row", "col", None), P("row", "col", None, None)),
        check_vma=False,
    )
```

profile of v0, /device:TPU:24, one launch (start us, length us, event | category | flops | bytes accessed | tf_op | source)
XLA Modules:
  0.0 48.8 jit_solution(11842939877239161919)
XLA Ops:
  0.6 0.0 copy-start
  0.6 0.9 %copy-done = bf16[4,128,256]{2,1,0:T(8,128)(2,1)S(1)} copy-done((bf16[4,128,256]{2,1,0:T(8,128)(2,1)S(1)}, bf16[4,128,256]{2,1,0:T(8,128)(2,1)}, u32[]{:S(2)}) %copy-start) | copy-done | bytes 262168
  1.6 0.0 copy-start.1
  1.6 0.8 %copy-done.1 = bf16[256,128]{1,0:T(8,128)(2,1)S(1)} copy-done((bf16[256,128]{1,0:T(8,128)(2,1)S(1)}, bf16[256,128]{1,0:T(8,128)(2,1)}, u32[]{:S(2)}) %copy-start.1) | copy-done | bytes 65560
  2.4 0.0 copy-start.2
  2.4 0.7 %copy-done.2 = s32[16]{0:T(128)S(1)} copy-done((s32[16]{0:T(128)S(1)}, s32[16]{0:T(128)}, u32[]{:S(2)}) %copy-start.2) | copy-done | bytes 88
  3.1 44.0 %shard_map.50 = (bf16[4,128,256]{2,1,0:T(8,128)(2,1)S(1)}, bf16[4,2,256,256]{3,2,1,0:T(8,128)(2,1)S(1)}) custom-call(s32[16]{0:T(128)S(1)} %copy-done.2, bf16[4,128,256]{2,1,0:T(8,128)(2,1)S(1)} %copy-done, bf16[256,128]{1,0:T(8,128)(2,1)S(1)} %copy-done.1), custom_call_target="tpu_custom_call" | custom-call | tf_op jit(solution)/shard_map/pallas_call | solution.py:415
  47.1 0.7 %copy.7 = bf16[4,128,256]{2,1,0:T(8,128)(2,1)} copy(bf16[4,128,256]{2,1,0:T(8,128)(2,1)S(1)} %get-tuple-element.4) | data formatting | bytes 524288
  47.8 1.0 %copy.8 = bf16[4,2,256,256]{3,2,1,0:T(8,128)(2,1)} copy(bf16[4,2,256,256]{3,2,1,0:T(8,128)(2,1)S(1)} %get-tuple-element.5) | data formatting | bytes 2097152
Async XLA Ops:
  0.6 1.0 %copy-start = (bf16[4,128,256]{2,1,0:T(8,128)(2,1)S(1)}, bf16[4,128,256]{2,1,0:T(8,128)(2,1)}, u32[]{:S(2)}) copy-start(bf16[4,128,256]{2,1,0:T(8,128)(2,1)} %p_hbm.1) | copy-start | bytes 786436
  1.6 0.8 %copy-start.1 = (bf16[256,128]{1,0:T(8,128)(2,1)S(1)}, bf16[256,128]{1,0:T(8,128)(2,1)}, u32[]{:S(2)}) copy-start(bf16[256,128]{1,0:T(8,128)(2,1)} %f_hbm.1) | copy-start | bytes 196612
  2.4 0.7 %copy-start.2 = (s32[16]{0:T(128)S(1)}, s32[16]{0:T(128)}, u32[]{:S(2)}) copy-start(s32[16]{0:T(128)} %ranks_hbm.1) | copy-start | bytes 196
where the time goes:
time: 49 us; the launch traced here: 48.8 us
  Pallas kernels  44 us (90%)
  local copies, waits for them, and re-layouts  4.11 us (8%)
  between operations  0.65 us (1%)
    pallas_call x1, Pallas kernels, on_device(): pl.pallas_call(functools.partial(kernel, rows, cols), out_shape=(jax.Shap...  44 us
    unnamed x8, local copies, waits for them, and re-layouts  4.11 us

commit v1 on v0

--- a/solution.py
+++ b/solution.py
@@ -213,11 +213,14 @@
     @pl.when(exists(c, z))
     def _():
         zf(z)
-        f_forward(0, z)
 
     from_source(0)
     for g in range(groups):
         p_forward(0, g)
+
+    @pl.when(exists(c, z))
+    def _():
+        f_forward(0, z)
 
     def near_first(body):
         for d in range(1, rows):

time: 49 us -> 49 us (level)
  no operation moved by 1% of the time
where the time goes in v1:
time: 49 us; the launch traced here: 48.8 us
  Pallas kernels  44 us (90%)
  local copies, waits for them, and re-layouts  4.11 us (8%)
  between operations  0.65 us (1%)
    pallas_call x1, Pallas kernels, on_device(): pl.pallas_call(functools.partial(kernel, rows, cols), out_shape=(jax.Shap...  44 us
    unnamed x8, local copies, waits for them, and re-layouts  4.11 us

profile of v1, /device:TPU:24, one launch (start us, length us, event | category | flops | bytes accessed | tf_op | source)
XLA Modules:
  0.0 48.8 jit_solution(2942416783467686067)
XLA Ops:
  0.6 0.0 copy-start
  0.6 0.9 %copy-done = bf16[4,128,256]{2,1,0:T(8,128)(2,1)S(1)} copy-done((bf16[4,128,256]{2,1,0:T(8,128)(2,1)S(1)}, bf16[4,128,256]{2,1,0:T(8,128)(2,1)}, u32[]{:S(2)}) %copy-start) | copy-done | bytes 262168
  1.6 0.0 copy-start.1
  1.6 0.8 %copy-done.1 = bf16[256,128]{1,0:T(8,128)(2,1)S(1)} copy-done((bf16[256,128]{1,0:T(8,128)(2,1)S(1)}, bf16[256,128]{1,0:T(8,128)(2,1)}, u32[]{:S(2)}) %copy-start.1) | copy-done | bytes 65560
  2.4 0.0 copy-start.2
  2.4 0.7 %copy-done.2 = s32[16]{0:T(128)S(1)} copy-done((s32[16]{0:T(128)S(1)}, s32[16]{0:T(128)}, u32[]{:S(2)}) %copy-start.2) | copy-done | bytes 88
  3.1 44.0 %shard_map.50 = (bf16[4,128,256]{2,1,0:T(8,128)(2,1)S(1)}, bf16[4,2,256,256]{3,2,1,0:T(8,128)(2,1)S(1)}) custom-call(s32[16]{0:T(128)S(1)} %copy-done.2, bf16[4,128,256]{2,1,0:T(8,128)(2,1)S(1)} %copy-done, bf16[256,128]{1,0:T(8,128)(2,1)S(1)} %copy-done.1), custom_call_target="tpu_custom_call" | custom-call | tf_op jit(solution)/shard_map/pallas_call | solution.py:418
  47.1 0.7 %copy.7 = bf16[4,128,256]{2,1,0:T(8,128)(2,1)} copy(bf16[4,128,256]{2,1,0:T(8,128)(2,1)S(1)} %get-tuple-element.4) | data formatting | bytes 524288
  47.8 1.0 %copy.8 = bf16[4,2,256,256]{3,2,1,0:T(8,128)(2,1)} copy(bf16[4,2,256,256]{3,2,1,0:T(8,128)(2,1)S(1)} %get-tuple-element.5) | data formatting | bytes 2097152
Async XLA Ops:
  0.6 1.0 %copy-start = (bf16[4,128,256]{2,1,0:T(8,128)(2,1)S(1)}, bf16[4,128,256]{2,1,0:T(8,128)(2,1)}, u32[]{:S(2)}) copy-start(bf16[4,128,256]{2,1,0:T(8,128)(2,1)} %p_hbm.1) | copy-start | bytes 786436
  1.6 0.8 %copy-start.1 = (bf16[256,128]{1,0:T(8,128)(2,1)S(1)}, bf16[256,128]{1,0:T(8,128)(2,1)}, u32[]{:S(2)}) copy-start(bf16[256,128]{1,0:T(8,128)(2,1)} %f_hbm.1) | copy-start | bytes 196612
  2.4 0.7 %copy-start.2 = (s32[16]{0:T(128)S(1)}, s32[16]{0:T(128)}, u32[]{:S(2)}) copy-start(s32[16]{0:T(128)} %ranks_hbm.1) | copy-start | bytes 196
